TPU v7x, 32 devices: a whole 2x2x4 slice. The times are simulated.
32 devices in a mesh: groups: 2 (over x), pair: 16 (over z, y, core).
Axes of the slice: x: 2, y: 2, z: 4, core: 2. Of those that a mesh axis runs over, the one named last changes fastest.
Arguments:
- amplitudes: bfloat16 [4096, 3600], P(('groups', 'pair')), parts along dimension 0, may hold values from -6 to 6
- pno_coef: bfloat16 [4096, 60, 256], P(('groups', 'pair')), parts along dimension 0, may hold values from -0.375 to 0.375
- metric: bfloat16 [512, 256], P('groups'), parts along dimension 0
- energies: float32 [4096, 60], P(('groups', 'pair')), parts along dimension 0, may hold values from 0.1 to 1
- pno_count: int32 [4096], P(('groups', 'pair')), parts along dimension 0, may hold values from 15 to 60, as said below
- cpl_self: int32 [8192], P(('groups', 'pair')), parts along dimension 0, may hold values from 0 to 127
- cpl_slot: int32 [8192], P(('groups', 'pair')), parts along dimension 0, may hold values from 0 to 63, as said below
- partner_list: int32 [2048], P(('groups', 'pair')), parts along dimension 0, may hold values from 0 to 2047, as said below
Outputs:
- residual: bfloat16 [4096, 3600], P(('groups', 'pair')), parts along dimension 0
There are 2 independent parts, one for each index of `groups`. A program takes and returns all parts, laid end to end along the dimension named above; each array names one. Nothing has to cross between parts.
Inputs may be any that keep to these rules, and one draw needn't show every extreme that they name: `pno_count`: every fragment has a pair with 60 natural orbitals. `cpl_slot`: every entry of a device's partner list is named by at least one of that device's couplings. `partner_list`: in each device's block of 64 entries, entry j * 4 + k names a pair owned by device j (its index // 128 is j), and the block's entries are distinct.
All inputs are finite; a program needn't handle non-finite values.
Results may differ from a plain program's by a relative error of at most 0.0065.
Values may be sent and summed in bfloat16 or wider, within the bound.
A program may use at most 128 MiB of HBM per device.

v0:
```python
import functools

import jax
import jax.numpy as jnp
from jax import lax
from jax.experimental import pallas as pl
from jax.experimental.pallas import tpu as pltpu
from jax.sharding import PartitionSpec as P

F32 = jnp.float32
BF16 = jnp.bfloat16
VMEM = pl.BlockSpec(memory_space=pltpu.VMEM)
SMEM = pl.BlockSpec(memory_space=pltpu.SMEM)
LIMIT = 60 * 1024 * 1024
WIDE = 64
LANES = 128
NT = (((1,), (1,)), ((), ()))


def halves(x):
    lane = lax.broadcasted_iota(jnp.int32, x.shape, 1)
    return jnp.where(lane < WIDE, x, 0.0), jnp.where(lane < WIDE, 0.0, x)


def kernel(
    peers, cap, width, group,
    count_s, self_s, slot_s, count_ref, self_ref, slot_ref, req_ref, en_ref, metric_ref, amp_ref, pno_ref,
    out_ref,
    asked_v, asked_s, amp32, vlo, vhi, tscr, v_ref, w_ref, t_ref, sendv, sendt, gotv, gott, ot_ref,
    sendr, gotr, ret32, own32, back32, hote, hoto, en64,
    local_sem, req_send, req_recv, vec_send, vec_recv, tile_send, tile_recv, back_send, back_recv,
):
    me = lax.axis_index("pair")
    pairs = count_ref.shape[1]
    domain = metric_ref.shape[0]
    couplings = self_ref.shape[1]
    slots = peers * cap
    batches = couplings // 2
    blocks = gott.shape[2] // LANES

    def peer(d):
        return lax.rem(me + d, peers)

    def remote(src, dst, send, recv, d):
        return pltpu.make_async_remote_copy(
            src_ref=src, dst_ref=dst, send_sem=send.at[d], recv_sem=recv.at[d],
            device_id={"pair": peer(d)}, device_id_type=pl.DeviceIdType.MESH,
        )

    def req_copy(d):
        return remote(req_ref.at[peer(d)], asked_v.at[me], req_send, req_recv, d)

    def vec_copy(d):
        return remote(
            sendv.at[pl.ds(peer(d) * cap, cap)], gotv.at[pl.ds(me * cap, cap)], vec_send, vec_recv, d
        )

    def tile_copy(d):
        return remote(sendt.at[peer(d)], gott.at[me], tile_send, tile_recv, d)

    def back_copy(d):
        return remote(sendr.at[peer(d)], gotr.at[me], back_send, back_recv, d)

    barrier = pltpu.get_barrier_semaphore()

    @pl.loop(1, peers)
    def _(d):
        pl.semaphore_signal(
            barrier, inc=1, device_id={"pair": peer(d)}, device_id_type=pl.DeviceIdType.MESH
        )

    pl.semaphore_wait(barrier, peers - 1)

    @pl.loop(1, peers)
    def _(d):
        req_copy(d).start()

    own_req = pltpu.make_async_copy(req_ref.at[me], asked_v.at[me], local_sem.at[0])
    own_req.start()

    for r in range(width):
        x = pno_ref[r].astype(F32)
        vlo[pl.ds(r * pairs, pairs), :] = x[:, :LANES]
        vhi[pl.ds(r * pairs, pairs), :] = x[:, LANES:]
    for r in range(width, WIDE):
        vlo[pl.ds(r * pairs, pairs), :] = jnp.zeros((pairs, LANES), F32)
        vhi[pl.ds(r * pairs, pairs), :] = jnp.zeros((pairs, LANES), F32)
    row = lax.broadcasted_iota(jnp.int32, (WIDE, LANES), 0)

    @pl.loop(0, pairs // 4)
    def _(g):
        for k in range(4):
            p = g * 4 + k
            live = row < count_s[p]
            lo = jnp.where(live, vlo[pl.ds(p, WIDE, stride=pairs), :], 0.0)
            hi = jnp.where(live, vhi[pl.ds(p, WIDE, stride=pairs), :], 0.0)
            v_ref[p, :, pl.ds(0, LANES)] = lo.astype(BF16)
            v_ref[p, :, pl.ds(LANES, LANES)] = hi.astype(BF16)

    rows = amp_ref.shape[0]
    amp32[pl.ds(0, rows), :] = amp_ref[...].astype(F32)
    amp32[pl.ds(rows, amp32.shape[0] - rows), :] = jnp.zeros((amp32.shape[0] - rows, pairs), F32)
    for r in range(WIDE):
        if r < width:
            x = amp32[pl.ds(r * width, WIDE), :]
            x = jnp.concatenate([x, x], axis=0).T
        else:
            x = jnp.zeros((pairs, LANES), F32)
        tscr[pl.ds(r * pairs, pairs), :] = x

    @pl.loop(0, pairs // 4)
    def _(g):
        for k in range(4):
            p = g * 4 + k
            left, right = halves(tscr[pl.ds(p, WIDE, stride=pairs), :])
            t_ref[2 * p] = left.astype(BF16)
            t_ref[2 * p + 1] = right.astype(BF16)

    @pl.loop(1, peers)
    def _(d):
        req_copy(d).wait()

    own_req.wait()
    to_scalar = pltpu.make_async_copy(asked_v, asked_s, local_sem.at[1])
    to_scalar.start()
    to_scalar.wait()

    def gather(to):
        for k in range(cap):
            sendv[to * cap + k] = v_ref[asked_s[to, k, 0]]
        for m in range(blocks):
            x = t_ref[2 * asked_s[to, 2 * m, 0]]
            if 2 * m + 1 < cap:
                x = x + t_ref[2 * asked_s[to, 2 * m + 1, 0] + 1]
            sendt[to, :, pl.ds(m * LANES, LANES)] = x

    @pl.loop(1, peers)
    def _(d):
        gather(peer(d))
        vec_copy(d).start()
        tile_copy(d).start()

    gather(me)
    own_vec = pltpu.make_async_copy(
        sendv.at[pl.ds(me * cap, cap)], gotv.at[pl.ds(me * cap, cap)], local_sem.at[0]
    )
    own_tile = pltpu.make_async_copy(sendt.at[me], gott.at[me], local_sem.at[1])
    own_vec.start()
    own_tile.start()

    metric = metric_ref[...]

    @pl.loop(0, pairs // 4)
    def _(g):
        v = v_ref[pl.ds(g * 4, 4)].reshape(4 * WIDE, domain)
        w = jnp.dot(v, metric, preferred_element_type=F32).astype(BF16)
        w_ref[pl.ds(g * 4, 4)] = w.reshape(4, WIDE, domain)

    lane = lax.broadcasted_iota(jnp.int32, (cap, LANES), 1)
    hote[...] = jnp.zeros_like(hote)
    hoto[...] = jnp.zeros_like(hoto)
    for j in range(peers):
        hit = jnp.where(asked_v[j] == lane, 1.0, 0.0)
        for k in range(cap):
            hot = hoto if k % 2 else hote
            hot[pl.ds(j * blocks + k // 2, 1), :] = hit[k : k + 1]
    en64[pl.ds(0, width), :] = en_ref[...]
    en64[pl.ds(width, WIDE - width), :] = jnp.zeros((WIDE - width, pairs), F32)

    @pl.loop(1, peers)
    def _(d):
        vec_copy(d).wait()
        tile_copy(d).wait()

    own_vec.wait()
    own_tile.wait()

    @pl.loop(0, peers)
    def _(j):
        for k in range(cap):
            x = gott[j, :, pl.ds((k // 2) * LANES, LANES)].astype(F32)
            swapped = pltpu.roll(x, WIDE, 1)
            here, there = (swapped, x) if k % 2 else (x, swapped)
            ot_ref[2 * (j * cap + k)] = halves(here)[0].astype(BF16)
            ot_ref[2 * (j * cap + k) + 1] = halves(there)[1].astype(BF16)

    own_z, ret_z = vlo, vhi
    side = 2 * WIDE
    diagonal = (lax.broadcasted_iota(jnp.int32, (side, side), 0) < WIDE) == (
        lax.broadcasted_iota(jnp.int32, (side, side), 1) < WIDE
    )

    @pl.loop(0, batches // group)
    def _(g):
        outs = []
        for k in range(group):
            i = g * group + k
            a1, a2 = self_s[i], self_s[i + batches]
            b1, b2 = slot_s[i], slot_s[i + batches]
            wa = jnp.concatenate([w_ref[a1], w_ref[a2]], axis=0)
            vb = jnp.concatenate([gotv[b1], gotv[b2]], axis=0)
            x = lax.dot_general(wa, vb, NT, preferred_element_type=F32)
            x = jnp.where(diagonal, x, 0.0)
            xt = x.T.astype(BF16)
            x = x.astype(BF16)
            tb = jnp.concatenate([ot_ref[2 * b1], ot_ref[2 * b2 + 1]], axis=0)
            ta = jnp.concatenate([t_ref[2 * a1], t_ref[2 * a2 + 1]], axis=0)
            left = jnp.dot(x, tb, preferred_element_type=F32).astype(BF16)
            proj = jnp.dot(xt, ta, preferred_element_type=F32).astype(BF16)
            to_own = jnp.dot(left, xt, preferred_element_type=F32)
            to_other = jnp.dot(proj, x, preferred_element_type=F32)
            outs.append((i, to_own[:WIDE] + to_own[WIDE:], to_other[:WIDE] + to_other[WIDE:]))
        for i, to_own, to_other in outs:
            own_z[pl.ds(i, WIDE, stride=batches), :] = to_own
            ret_z[pl.ds(i, WIDE, stride=batches), :] = to_other

    hs = lax.broadcasted_iota(jnp.int32, (slots, couplings), 0) == slot_ref[...]
    hs = jnp.where(hs, 1.0, 0.0)
    hs = jnp.concatenate([hs[:, :batches], hs[:, batches:]], axis=0).astype(BF16)
    for r in range(WIDE):
        z = ret_z[pl.ds(r * batches, batches), :].astype(BF16)
        y = jnp.dot(hs, z, preferred_element_type=F32)
        ret32[pl.ds(r * slots, slots), :] = halves(y[:slots])[0] + halves(y[slots:])[1]

    def pack(to):
        for m in range(blocks):
            x = ret32[pl.ds(to * cap + 2 * m, WIDE, stride=slots), :]
            x = halves(x + pltpu.roll(x, WIDE, 1))[0]
            if 2 * m + 1 < cap:
                y = ret32[pl.ds(to * cap + 2 * m + 1, WIDE, stride=slots), :]
                x = x + halves(y + pltpu.roll(y, WIDE, 1))[1]
            sendr[to, :, pl.ds(m * LANES, LANES)] = x.astype(BF16)

    @pl.loop(1, peers)
    def _(d):
        pack(peer(d))
        back_copy(d).start()

    pack(me)
    own_back = pltpu.make_async_copy(sendr.at[me], gotr.at[me], local_sem.at[0])
    own_back.start()

    ho = lax.broadcasted_iota(jnp.int32, (pairs, couplings), 0) == self_ref[...]
    ho = jnp.where(ho, 1.0, 0.0).astype(BF16)
    for r in range(width):
        z = own_z[pl.ds(r * batches, batches), :].T
        z = jnp.concatenate([z[:WIDE], z[WIDE:]], axis=1).astype(BF16)
        own32[pl.ds(r * WIDE, WIDE), :] = lax.dot_general(z, ho, NT, preferred_element_type=F32)

    @pl.loop(1, peers)
    def _(d):
        back_copy(d).wait()

    own_back.wait()

    @pl.loop(0, peers)
    def _(j):
        for m in range(blocks):
            back32[pl.ds((j * blocks + m) * WIDE, WIDE), :] = gotr[
                j, :, pl.ds(m * LANES, LANES)
            ].astype(F32)

    hot_even = hote[...].astype(BF16)
    hot_odd = hoto[...].astype(BF16)
    count = count_ref[...]
    inside = lax.broadcasted_iota(jnp.int32, (WIDE, pairs), 0) < count
    en = en64[...]
    out32 = tscr
    for r in range(width):
        x = back32[pl.ds(r, peers * blocks, stride=WIDE), :].T.astype(BF16)
        y = jnp.dot(x[:WIDE], hot_even, preferred_element_type=F32)
        y = y + jnp.dot(x[WIDE:], hot_odd, preferred_element_type=F32)
        y = y + own32[pl.ds(r * WIDE, WIDE), :]
        z = (en + en[r : r + 1]) * amp32[pl.ds(r * width, WIDE), :] - y
        out32[pl.ds(r * width, WIDE), :] = jnp.where(inside & (r < count), z, 0.0)
    out_ref[...] = out32[pl.ds(0, rows), :].astype(BF16)


def per_device(amplitudes, pno_coef, metric, energies, pno_count, cpl_self, cpl_slot, partner_list):
    peers = lax.axis_size("pair")
    pairs, tile_size = amplitudes.shape
    width = energies.shape[1]
    domain = pno_coef.shape[2]
    couplings = cpl_self.shape[0]
    slots = partner_list.shape[0]
    cap = slots // peers
    blocks = -(-cap // 2)
    requests = jnp.broadcast_to(
        lax.rem(partner_list, pairs).reshape(peers, cap, 1), (peers, cap, LANES)
    )
    out = pl.pallas_call(
        functools.partial(kernel, peers, cap, width, 4),
        out_shape=jax.ShapeDtypeStruct((tile_size, pairs), BF16),
        in_specs=[SMEM] * 3 + [VMEM] * 8,
        out_specs=VMEM,
        scratch_shapes=[
            pltpu.VMEM((peers, cap, LANES), jnp.int32),
            pltpu.SMEM((peers, cap, LANES), jnp.int32),
            pltpu.VMEM((tile_size + 16, pairs), F32),
            pltpu.VMEM((WIDE * pairs, LANES), F32),
            pltpu.VMEM((WIDE * pairs, LANES), F32),
            pltpu.VMEM((WIDE * pairs, LANES), F32),
            pltpu.VMEM((pairs, WIDE, domain), BF16),
            pltpu.VMEM((pairs, WIDE, domain), BF16),
            pltpu.VMEM((2 * pairs, WIDE, LANES), BF16),
            pltpu.VMEM((slots, WIDE, domain), BF16),
            pltpu.VMEM((peers, WIDE, blocks * LANES), BF16),
            pltpu.VMEM((slots, WIDE, domain), BF16),
            pltpu.VMEM((peers, WIDE, blocks * LANES), BF16),
            pltpu.VMEM((2 * slots, WIDE, LANES), BF16),
            pltpu.VMEM((peers, WIDE, blocks * LANES), BF16),
            pltpu.VMEM((peers, WIDE, blocks * LANES), BF16),
            pltpu.VMEM((WIDE * slots, LANES), F32),
            pltpu.VMEM((WIDE * WIDE, pairs), F32),
            pltpu.VMEM((WIDE * peers * blocks, LANES), F32),
            pltpu.VMEM((peers * blocks, LANES), F32),
            pltpu.VMEM((peers * blocks, LANES), F32),
            pltpu.VMEM((WIDE, pairs), F32),
            pltpu.SemaphoreType.DMA((2,)),
        ]
        + [pltpu.SemaphoreType.DMA((peers,))] * 8,
        compiler_params=pltpu.CompilerParams(
            vmem_limit_bytes=LIMIT, collective_id=0, has_side_effects=True
        ),
    )(
        pno_count, cpl_self, cpl_slot,
        pno_count.reshape(1, pairs), cpl_self.reshape(1, couplings), cpl_slot.reshape(1, couplings),
        requests, energies.T, metric, amplitudes.T, pno_coef.transpose(1, 0, 2),
    )
    return out.T


def solution(mesh):
    return jax.shard_map(
        per_device,
        mesh=mesh,
        in_specs=(
            P(("groups", "pair"), None),
            P(("groups", "pair"), None, None),
            P("groups", None),
            P(("groups", "pair"), None),
            P(("groups", "pair")),
            P(("groups", "pair")),
            P(("groups", "pair")),
            P(("groups", "pair")),
        ),
        out_specs=P(("groups", "pair"), None),
        check_vma=False,
    )
```

profile of v0, /device:TPU:0, one launch (start us, length us, event | category | flops | bytes accessed | tf_op | source)
XLA Modules:
  0.0 139.4 jit_solution(8067186070528407361)
XLA Ops:
  0.0 0.7 compare_select_fusion
  0.7 0.1 broadcast_in_dim.7
  0.7 0.7 broadcast_in_dim.8.req_ref
  1.5 135.8 %shard_map.82 = bf16[3600,128]{1,0:T(8,128)(2,1)} custom-call(s32[128]{0:T(128)} %count_s.1, s32[256]{0:T(256)} %self_s.1, s32[256]{0:T(256)} %slot_s.1, s32[1,128]{1,0:T(1,128)} %bitcast.13, s32[1,256]{1,0:T(1,128)} %bitcast.11, s32[1,256]{1,0:T(1,128)} %bitcast.12, s32[16,4,128]{2,1,0:T(4,128)} %broadcast_in_dim.8.req_ref, f32[60,128]{1,0:T(8,128)} %bitcast.10, ...), custom_call_target="tpu_custom_call" | custom-call | tf_op jit(solution)/shard_map/pallas_call | solution.py:291
  137.2 2.2 %copy.10 = bf16[128,3600]{0,1:T(8,128)(2,1)} copy(bf16[128,3600]{0,1:T(8,128)(2,1)} %bitcast.8) | data formatting | bytes 1843200
where the time goes:
time: 142 us; the launch traced here: 139 us
  Pallas kernels  136 us (96%)
  local copies, waits for them, and re-layouts  2.95 us (2%)
    pallas_call x1, Pallas kernels, per_device(): pl.pallas_call(functools.partial(kernel, peers, cap, width, 4), out_shape...  136 us

commit v1 on v0

--- a/solution.py
+++ b/solution.py
@@ -13,6 +13,7 @@
 SMEM = pl.BlockSpec(memory_space=pltpu.SMEM)
 LIMIT = 60 * 1024 * 1024
 WIDE = 64
+SKEW = 8
 LANES = 128
 NT = (((1,), (1,)), ((), ()))
 
@@ -37,6 +38,10 @@
     slots = peers * cap
     batches = couplings // 2
     blocks = gott.shape[2] // LANES
+    pitch = pairs + SKEW
+    bpitch = batches + SKEW
+    spitch = slots + SKEW
+    wpitch = WIDE + SKEW
 
     def peer(d):
         return lax.rem(me + d, peers)
@@ -80,11 +85,11 @@
 
     for r in range(width):
         x = pno_ref[r].astype(F32)
-        vlo[pl.ds(r * pairs, pairs), :] = x[:, :LANES]
-        vhi[pl.ds(r * pairs, pairs), :] = x[:, LANES:]
+        vlo[pl.ds(r * pitch, pairs), :] = x[:, :LANES]
+        vhi[pl.ds(r * pitch, pairs), :] = x[:, LANES:]
     for r in range(width, WIDE):
-        vlo[pl.ds(r * pairs, pairs), :] = jnp.zeros((pairs, LANES), F32)
-        vhi[pl.ds(r * pairs, pairs), :] = jnp.zeros((pairs, LANES), F32)
+        vlo[pl.ds(r * pitch, pairs), :] = jnp.zeros((pairs, LANES), F32)
+        vhi[pl.ds(r * pitch, pairs), :] = jnp.zeros((pairs, LANES), F32)
     row = lax.broadcasted_iota(jnp.int32, (WIDE, LANES), 0)
 
     @pl.loop(0, pairs // 4)
@@ -92,10 +97,42 @@
         for k in range(4):
             p = g * 4 + k
             live = row < count_s[p]
-            lo = jnp.where(live, vlo[pl.ds(p, WIDE, stride=pairs), :], 0.0)
-            hi = jnp.where(live, vhi[pl.ds(p, WIDE, stride=pairs), :], 0.0)
+            lo = jnp.where(live, vlo[pl.ds(p, WIDE, stride=pitch), :], 0.0)
+            hi = jnp.where(live, vhi[pl.ds(p, WIDE, stride=pitch), :], 0.0)
             v_ref[p, :, pl.ds(0, LANES)] = lo.astype(BF16)
             v_ref[p, :, pl.ds(LANES, LANES)] = hi.astype(BF16)
+
+    @pl.loop(1, peers)
+    def _(d):
+        req_copy(d).wait()
+
+    own_req.wait()
+    to_scalar = pltpu.make_async_copy(asked_v, asked_s, local_sem.at[1])
+    to_scalar.start()
+    to_scalar.wait()
+
+    def take_vectors(to):
+        for k in range(cap):
+            sendv[to * cap + k] = v_ref[asked_s[to, k, 0]]
+
+    def take_tiles(to):
+        for m in range(blocks):
+            x = t_ref[2 * asked_s[to, 2 * m, 0]]
+            if 2 * m + 1 < cap:
+                x = x + t_ref[2 * asked_s[to, 2 * m + 1, 0] + 1]
+            sendt[to, :, pl.ds(m * LANES, LANES)] = x
+
+    @pl.loop(1, peers)
+    def _(d):
+        d = 1 + lax.rem(d + peers // 2 - 2, peers - 1)
+        take_vectors(peer(d))
+        vec_copy(d).start()
+
+    take_vectors(me)
+    own_vec = pltpu.make_async_copy(
+        sendv.at[pl.ds(me * cap, cap)], gotv.at[pl.ds(me * cap, cap)], local_sem.at[0]
+    )
+    own_vec.start()
 
     rows = amp_ref.shape[0]
     amp32[pl.ds(0, rows), :] = amp_ref[...].astype(F32)
@@ -106,46 +143,24 @@
             x = jnp.concatenate([x, x], axis=0).T
         else:
             x = jnp.zeros((pairs, LANES), F32)
-        tscr[pl.ds(r * pairs, pairs), :] = x
+        tscr[pl.ds(r * pitch, pairs), :] = x
 
     @pl.loop(0, pairs // 4)
     def _(g):
         for k in range(4):
             p = g * 4 + k
-            left, right = halves(tscr[pl.ds(p, WIDE, stride=pairs), :])
+            left, right = halves(tscr[pl.ds(p, WIDE, stride=pitch), :])
             t_ref[2 * p] = left.astype(BF16)
             t_ref[2 * p + 1] = right.astype(BF16)
 
     @pl.loop(1, peers)
     def _(d):
-        req_copy(d).wait()
-
-    own_req.wait()
-    to_scalar = pltpu.make_async_copy(asked_v, asked_s, local_sem.at[1])
-    to_scalar.start()
-    to_scalar.wait()
-
-    def gather(to):
-        for k in range(cap):
-            sendv[to * cap + k] = v_ref[asked_s[to, k, 0]]
-        for m in range(blocks):
-            x = t_ref[2 * asked_s[to, 2 * m, 0]]
-            if 2 * m + 1 < cap:
-                x = x + t_ref[2 * asked_s[to, 2 * m + 1, 0] + 1]
-            sendt[to, :, pl.ds(m * LANES, LANES)] = x
-
-    @pl.loop(1, peers)
-    def _(d):
-        gather(peer(d))
-        vec_copy(d).start()
+        d = 1 + lax.rem(d + peers // 2 - 2, peers - 1)
+        take_tiles(peer(d))
         tile_copy(d).start()
 
-    gather(me)
-    own_vec = pltpu.make_async_copy(
-        sendv.at[pl.ds(me * cap, cap)], gotv.at[pl.ds(me * cap, cap)], local_sem.at[0]
-    )
+    take_tiles(me)
     own_tile = pltpu.make_async_copy(sendt.at[me], gott.at[me], local_sem.at[1])
-    own_vec.start()
     own_tile.start()
 
     metric = metric_ref[...]
@@ -201,8 +216,8 @@
             vb = jnp.concatenate([gotv[b1], gotv[b2]], axis=0)
             x = lax.dot_general(wa, vb, NT, preferred_element_type=F32)
             x = jnp.where(diagonal, x, 0.0)
-            xt = x.T.astype(BF16)
             x = x.astype(BF16)
+            xt = x.T
             tb = jnp.concatenate([ot_ref[2 * b1], ot_ref[2 * b2 + 1]], axis=0)
             ta = jnp.concatenate([t_ref[2 * a1], t_ref[2 * a2 + 1]], axis=0)
             left = jnp.dot(x, tb, preferred_element_type=F32).astype(BF16)
@@ -211,23 +226,23 @@
             to_other = jnp.dot(proj, x, preferred_element_type=F32)
             outs.append((i, to_own[:WIDE] + to_own[WIDE:], to_other[:WIDE] + to_other[WIDE:]))
         for i, to_own, to_other in outs:
-            own_z[pl.ds(i, WIDE, stride=batches), :] = to_own
-            ret_z[pl.ds(i, WIDE, stride=batches), :] = to_other
+            own_z[pl.ds(i, WIDE, stride=bpitch), :] = to_own
+            ret_z[pl.ds(i, WIDE, stride=bpitch), :] = to_other
 
     hs = lax.broadcasted_iota(jnp.int32, (slots, couplings), 0) == slot_ref[...]
     hs = jnp.where(hs, 1.0, 0.0)
     hs = jnp.concatenate([hs[:, :batches], hs[:, batches:]], axis=0).astype(BF16)
     for r in range(WIDE):
-        z = ret_z[pl.ds(r * batches, batches), :].astype(BF16)
+        z = ret_z[pl.ds(r * bpitch, batches), :].astype(BF16)
         y = jnp.dot(hs, z, preferred_element_type=F32)
-        ret32[pl.ds(r * slots, slots), :] = halves(y[:slots])[0] + halves(y[slots:])[1]
+        ret32[pl.ds(r * spitch, slots), :] = halves(y[:slots])[0] + halves(y[slots:])[1]
 
     def pack(to):
         for m in range(blocks):
-            x = ret32[pl.ds(to * cap + 2 * m, WIDE, stride=slots), :]
+            x = ret32[pl.ds(to * cap + 2 * m, WIDE, stride=spitch), :]
             x = halves(x + pltpu.roll(x, WIDE, 1))[0]
             if 2 * m + 1 < cap:
-                y = ret32[pl.ds(to * cap + 2 * m + 1, WIDE, stride=slots), :]
+                y = ret32[pl.ds(to * cap + 2 * m + 1, WIDE, stride=spitch), :]
                 x = x + halves(y + pltpu.roll(y, WIDE, 1))[1]
             sendr[to, :, pl.ds(m * LANES, LANES)] = x.astype(BF16)
 
@@ -243,7 +258,7 @@
     ho = lax.broadcasted_iota(jnp.int32, (pairs, couplings), 0) == self_ref[...]
     ho = jnp.where(ho, 1.0, 0.0).astype(BF16)
     for r in range(width):
-        z = own_z[pl.ds(r * batches, batches), :].T
+        z = own_z[pl.ds(r * bpitch, batches), :].T
         z = jnp.concatenate([z[:WIDE], z[WIDE:]], axis=1).astype(BF16)
         own32[pl.ds(r * WIDE, WIDE), :] = lax.dot_general(z, ho, NT, preferred_element_type=F32)
 
@@ -256,7 +271,7 @@
     @pl.loop(0, peers)
     def _(j):
         for m in range(blocks):
-            back32[pl.ds((j * blocks + m) * WIDE, WIDE), :] = gotr[
+            back32[pl.ds((j * blocks + m) * wpitch, WIDE), :] = gotr[
                 j, :, pl.ds(m * LANES, LANES)
             ].astype(F32)
 
@@ -267,7 +282,7 @@
     en = en64[...]
     out32 = tscr
     for r in range(width):
-        x = back32[pl.ds(r, peers * blocks, stride=WIDE), :].T.astype(BF16)
+        x = back32[pl.ds(r, peers * blocks, stride=wpitch), :].T.astype(BF16)
         y = jnp.dot(x[:WIDE], hot_even, preferred_element_type=F32)
         y = y + jnp.dot(x[WIDE:], hot_odd, preferred_element_type=F32)
         y = y + own32[pl.ds(r * WIDE, WIDE), :]
@@ -289,7 +304,7 @@
         lax.rem(partner_list, pairs).reshape(peers, cap, 1), (peers, cap, LANES)
     )
     out = pl.pallas_call(
-        functools.partial(kernel, peers, cap, width, 4),
+        functools.partial(kernel, peers, cap, width, 16),
         out_shape=jax.ShapeDtypeStruct((tile_size, pairs), BF16),
         in_specs=[SMEM] * 3 + [VMEM] * 8,
         out_specs=VMEM,
@@ -297,9 +312,9 @@
             pltpu.VMEM((peers, cap, LANES), jnp.int32),
             pltpu.SMEM((peers, cap, LANES), jnp.int32),
             pltpu.VMEM((tile_size + 16, pairs), F32),
-            pltpu.VMEM((WIDE * pairs, LANES), F32),
-            pltpu.VMEM((WIDE * pairs, LANES), F32),
-            pltpu.VMEM((WIDE * pairs, LANES), F32),
+            pltpu.VMEM((WIDE * (max(pairs, couplings // 2) + SKEW), LANES), F32),
+            pltpu.VMEM((WIDE * (max(pairs, couplings // 2) + SKEW), LANES), F32),
+            pltpu.VMEM((WIDE * (max(pairs, couplings // 2) + SKEW), LANES), F32),
             pltpu.VMEM((pairs, WIDE, domain), BF16),
             pltpu.VMEM((pairs, WIDE, domain), BF16),
             pltpu.VMEM((2 * pairs, WIDE, LANES), BF16),
@@ -310,9 +325,9 @@
             pltpu.VMEM((2 * slots, WIDE, LANES), BF16),
             pltpu.VMEM((peers, WIDE, blocks * LANES), BF16),
             pltpu.VMEM((peers, WIDE, blocks * LANES), BF16),
-            pltpu.VMEM((WIDE * slots, LANES), F32),
+            pltpu.VMEM((WIDE * (slots + SKEW), LANES), F32),
             pltpu.VMEM((WIDE * WIDE, pairs), F32),
-            pltpu.VMEM((WIDE * peers * blocks, LANES), F32),
+            pltpu.VMEM(((WIDE + SKEW) * peers * blocks, LANES), F32),
             pltpu.VMEM((peers * blocks, LANES), F32),
             pltpu.VMEM((peers * blocks, LANES), F32),
             pltpu.VMEM((WIDE, pairs), F32),

time: 142 us -> 127 us (0.89); the launches traced: 139 us -> 127 us
  Pallas kernels: 136 us -> 123 us
    pallas_call x1, Pallas kernels: 136 us -> 123 us  [per_device(): pl.pallas_call(functools.partial(kernel, peers, cap, width, 16), out_shap...]
where the time goes in v1:
time: 127 us
  Pallas kernels  123 us (97%)
  local copies, waits for them, and re-layouts  2.95 us (2%)
    pallas_call x1, Pallas kernels, per_device(): pl.pallas_call(functools.partial(kernel, peers, cap, width, 16), out_shap...  123 us

profile of v1, /device:TPU:0, one launch (start us, length us, event | category | flops | bytes accessed | tf_op | source)
XLA Modules:
  0.0 126.6 jit_solution(11358026285468904755)
XLA Ops:
  0.0 0.7 compare_select_fusion
  0.7 0.1 broadcast_in_dim.7
  0.7 0.7 broadcast_in_dim.8.req_ref
  1.5 123.0 %shard_map.82 = bf16[3600,128]{1,0:T(8,128)(2,1)} custom-call(s32[128]{0:T(128)} %count_s.1, s32[256]{0:T(256)} %self_s.1, s32[256]{0:T(256)} %slot_s.1, s32[1,128]{1,0:T(1,128)} %bitcast.13, s32[1,256]{1,0:T(1,128)} %bitcast.11, s32[1,256]{1,0:T(1,128)} %bitcast.12, s32[16,4,128]{2,1,0:T(4,128)} %broadcast_in_dim.8.req_ref, f32[60,128]{1,0:T(8,128)} %bitcast.10, ...), custom_call_target="tpu_custom_call" | custom-call | tf_op jit(solution)/shard_map/pallas_call | solution.py:306
  124.4 2.2 %copy.10 = bf16[128,3600]{0,1:T(8,128)(2,1)} copy(bf16[128,3600]{0,1:T(8,128)(2,1)} %bitcast.8) | data formatting | bytes 1843200

commit v2 on v1

--- a/solution.py
+++ b/solution.py
@@ -28,7 +28,7 @@
     count_s, self_s, slot_s, count_ref, self_ref, slot_ref, req_ref, en_ref, metric_ref, amp_ref, pno_ref,
     out_ref,
     asked_v, asked_s, amp32, vlo, vhi, tscr, v_ref, w_ref, t_ref, sendv, sendt, gotv, gott, ot_ref,
-    sendr, gotr, ret32, own32, back32, hote, hoto, en64,
+    sendr, gotr, ret32, own32, back32, hote, hoto, en64, x_ref,
     local_sem, req_send, req_recv, vec_send, vec_recv, tile_send, tile_recv, back_send, back_recv,
 ):
     me = lax.axis_index("pair")
@@ -185,9 +185,64 @@
     @pl.loop(1, peers)
     def _(d):
         vec_copy(d).wait()
+
+    own_vec.wait()
+
+    own_z, ret_z = vlo, vhi
+    side = 2 * WIDE
+    diagonal = (lax.broadcasted_iota(jnp.int32, (side, side), 0) < WIDE) == (
+        lax.broadcasted_iota(jnp.int32, (side, side), 1) < WIDE
+    )
+
+    @pl.loop(0, batches // group)
+    def _(g):
+        outs = []
+        for k in range(group):
+            i = g * group + k
+            a1, a2 = self_s[i], self_s[i + batches]
+            b1, b2 = slot_s[i], slot_s[i + batches]
+            wa = jnp.concatenate([w_ref[a1], w_ref[a2]], axis=0)
+            vb = jnp.concatenate([gotv[b1], gotv[b2]], axis=0)
+            x = lax.dot_general(wa, vb, NT, preferred_element_type=F32)
+            x = jnp.where(diagonal, x, 0.0).astype(BF16)
+            ta = jnp.concatenate([t_ref[2 * a1], t_ref[2 * a2 + 1]], axis=0)
+            proj = jnp.dot(x.T, ta, preferred_element_type=F32).astype(BF16)
+            to_other = jnp.dot(proj, x, preferred_element_type=F32)
+            outs.append((i, x, to_other[:WIDE] + to_other[WIDE:]))
+        for i, x, to_other in outs:
+            x_ref[i] = x
+            ret_z[pl.ds(i, WIDE, stride=bpitch), :] = to_other
+
+    hs = lax.broadcasted_iota(jnp.int32, (slots, couplings), 0) == slot_ref[...]
+    hs = jnp.where(hs, 1.0, 0.0)
+    hs = jnp.concatenate([hs[:, :batches], hs[:, batches:]], axis=0).astype(BF16)
+    for r in range(WIDE):
+        z = ret_z[pl.ds(r * bpitch, batches), :].astype(BF16)
+        y = jnp.dot(hs, z, preferred_element_type=F32)
+        ret32[pl.ds(r * spitch, slots), :] = halves(y[:slots])[0] + halves(y[slots:])[1]
+
+    def pack(to):
+        for m in range(blocks):
+            x = ret32[pl.ds(to * cap + 2 * m, WIDE, stride=spitch), :]
+            x = halves(x + pltpu.roll(x, WIDE, 1))[0]
+            if 2 * m + 1 < cap:
+                y = ret32[pl.ds(to * cap + 2 * m + 1, WIDE, stride=spitch), :]
+                x = x + halves(y + pltpu.roll(y, WIDE, 1))[1]
+            sendr[to, :, pl.ds(m * LANES, LANES)] = x.astype(BF16)
+
+    @pl.loop(1, peers)
+    def _(d):
+        pack(peer(d))
+        back_copy(d).start()
+
+    pack(me)
+    own_back = pltpu.make_async_copy(sendr.at[me], gotr.at[me], local_sem.at[2])
+    own_back.start()
+
+    @pl.loop(1, peers)
+    def _(d):
         tile_copy(d).wait()
 
-    own_vec.wait()
     own_tile.wait()
 
     @pl.loop(0, peers)
@@ -199,61 +254,19 @@
             ot_ref[2 * (j * cap + k)] = halves(here)[0].astype(BF16)
             ot_ref[2 * (j * cap + k) + 1] = halves(there)[1].astype(BF16)
 
-    own_z, ret_z = vlo, vhi
-    side = 2 * WIDE
-    diagonal = (lax.broadcasted_iota(jnp.int32, (side, side), 0) < WIDE) == (
-        lax.broadcasted_iota(jnp.int32, (side, side), 1) < WIDE
-    )
-
     @pl.loop(0, batches // group)
     def _(g):
         outs = []
         for k in range(group):
             i = g * group + k
-            a1, a2 = self_s[i], self_s[i + batches]
             b1, b2 = slot_s[i], slot_s[i + batches]
-            wa = jnp.concatenate([w_ref[a1], w_ref[a2]], axis=0)
-            vb = jnp.concatenate([gotv[b1], gotv[b2]], axis=0)
-            x = lax.dot_general(wa, vb, NT, preferred_element_type=F32)
-            x = jnp.where(diagonal, x, 0.0)
-            x = x.astype(BF16)
-            xt = x.T
+            x = x_ref[i]
             tb = jnp.concatenate([ot_ref[2 * b1], ot_ref[2 * b2 + 1]], axis=0)
-            ta = jnp.concatenate([t_ref[2 * a1], t_ref[2 * a2 + 1]], axis=0)
             left = jnp.dot(x, tb, preferred_element_type=F32).astype(BF16)
-            proj = jnp.dot(xt, ta, preferred_element_type=F32).astype(BF16)
-            to_own = jnp.dot(left, xt, preferred_element_type=F32)
-            to_other = jnp.dot(proj, x, preferred_element_type=F32)
-            outs.append((i, to_own[:WIDE] + to_own[WIDE:], to_other[:WIDE] + to_other[WIDE:]))
-        for i, to_own, to_other in outs:
+            to_own = lax.dot_general(left, x, NT, preferred_element_type=F32)
+            outs.append((i, to_own[:WIDE] + to_own[WIDE:]))
+        for i, to_own in outs:
             own_z[pl.ds(i, WIDE, stride=bpitch), :] = to_own
-            ret_z[pl.ds(i, WIDE, stride=bpitch), :] = to_other
-
-    hs = lax.broadcasted_iota(jnp.int32, (slots, couplings), 0) == slot_ref[...]
-    hs = jnp.where(hs, 1.0, 0.0)
-    hs = jnp.concatenate([hs[:, :batches], hs[:, batches:]], axis=0).astype(BF16)
-    for r in range(WIDE):
-        z = ret_z[pl.ds(r * bpitch, batches), :].astype(BF16)
-        y = jnp.dot(hs, z, preferred_element_type=F32)
-        ret32[pl.ds(r * spitch, slots), :] = halves(y[:slots])[0] + halves(y[slots:])[1]
-
-    def pack(to):
-        for m in range(blocks):
-            x = ret32[pl.ds(to * cap + 2 * m, WIDE, stride=spitch), :]
-            x = halves(x + pltpu.roll(x, WIDE, 1))[0]
-            if 2 * m + 1 < cap:
-                y = ret32[pl.ds(to * cap + 2 * m + 1, WIDE, stride=spitch), :]
-                x = x + halves(y + pltpu.roll(y, WIDE, 1))[1]
-            sendr[to, :, pl.ds(m * LANES, LANES)] = x.astype(BF16)
-
-    @pl.loop(1, peers)
-    def _(d):
-        pack(peer(d))
-        back_copy(d).start()
-
-    pack(me)
-    own_back = pltpu.make_async_copy(sendr.at[me], gotr.at[me], local_sem.at[0])
-    own_back.start()
 
     ho = lax.broadcasted_iota(jnp.int32, (pairs, couplings), 0) == self_ref[...]
     ho = jnp.where(ho, 1.0, 0.0).astype(BF16)
@@ -331,7 +344,8 @@
             pltpu.VMEM((peers * blocks, LANES), F32),
             pltpu.VMEM((peers * blocks, LANES), F32),
             pltpu.VMEM((WIDE, pairs), F32),
-            pltpu.SemaphoreType.DMA((2,)),
+            pltpu.VMEM((couplings // 2, 2 * WIDE, 2 * WIDE), BF16),
+            pltpu.SemaphoreType.DMA((3,)),
         ]
         + [pltpu.SemaphoreType.DMA((peers,))] * 8,
         compiler_params=pltpu.CompilerParams(

time: 127 us -> 111 us (0.87)
  Pallas kernels: 123 us -> 106 us
    pallas_call x1, Pallas kernels: 123 us -> 106 us  [per_device(): pl.pallas_call(functools.partial(kernel, peers, cap, width, 16), out_shap...]
where the time goes in v2:
time: 111 us; the launch traced here: 110 us
  Pallas kernels  106 us (95%)
  local copies, waits for them, and re-layouts  2.95 us (3%)
    pallas_call x1, Pallas kernels, per_device(): pl.pallas_call(functools.partial(kernel, peers, cap, width, 16), out_shap...  106 us

profile of v2, /device:TPU:0, one launch (start us, length us, event | category | flops | bytes accessed | tf_op | source)
XLA Modules:
  0.0 109.5 jit_solution(15396422145124542973)
XLA Ops:
  0.0 0.7 compare_select_fusion
  0.7 0.1 broadcast_in_dim.7
  0.7 0.7 broadcast_in_dim.8.req_ref
  1.5 105.9 %shard_map.82 = bf16[3600,128]{1,0:T(8,128)(2,1)} custom-call(s32[128]{0:T(128)} %count_s.1, s32[256]{0:T(256)} %self_s.1, s32[256]{0:T(256)} %slot_s.1, s32[1,128]{1,0:T(1,128)} %bitcast.13, s32[1,256]{1,0:T(1,128)} %bitcast.11, s32[1,256]{1,0:T(1,128)} %bitcast.12, s32[16,4,128]{2,1,0:T(4,128)} %broadcast_in_dim.8.req_ref, f32[60,128]{1,0:T(8,128)} %bitcast.10, ...), custom_call_target="tpu_custom_call" | custom-call | tf_op jit(solution)/shard_map/pallas_call | solution.py:319
  107.3 2.2 %copy.10 = bf16[128,3600]{0,1:T(8,128)(2,1)} copy(bf16[128,3600]{0,1:T(8,128)(2,1)} %bitcast.8) | data formatting | bytes 1843200
